TPU v7x, 32 devices: a whole 2x2x4 slice. The times are simulated.
32 devices in a mesh: groups: 2 (over y), wloop: 4 (over z), items: 4 (over x, core).
Axes of the slice: x: 2, y: 2, z: 4, core: 2. Of those that a mesh axis runs over, the one named last changes fastest.
Arguments:
- features: bfloat16 [2048, 16384], P(('groups', 'items'), 'wloop'), parts along dimension 0, may hold values from -6 to 6
- cotangent: bfloat16 [2048, 16384], P(('groups', 'items'), 'wloop'), parts along dimension 0, may hold values from -6 to 6
- block_weights: bfloat16 [256, 256, 256], P('wloop'), may hold values from -0.1875 to 0.1875
- block_rows: int32 [256], P('wloop'), may hold values from 0 to 63, as said below
- block_cols: int32 [256], P('wloop'), may hold values from 0 to 63, as said below
- lowrank_in: bfloat16 [128, 16384], P(None, 'wloop'), may hold values from -0.046875 to 0.046875
- lowrank_out: bfloat16 [128, 16384], P(None, 'wloop'), may hold values from -0.5 to 0.5
Outputs:
- mixed: bfloat16 [2048, 16384], P(('groups', 'items'), 'wloop'), parts along dimension 0
- block_grads: float32 [512, 256, 256], P(('groups', 'items'), 'wloop'), parts along dimension 0
- grad_in: float32 [256, 16384], P(('groups', 'items'), 'wloop'), parts along dimension 0
- grad_out: float32 [256, 16384], P(('groups', 'items'), 'wloop'), parts along dimension 0
There are 2 independent parts, one for each index of `groups`. A program takes and returns all parts, laid end to end along the dimension named above; an argument that names none is the same for every part. Nothing has to cross between parts.
Inputs may be any that keep to these rules, and one draw needn't show every extreme that they name: `block_rows`: the stored blocks form a strided block pattern: every input block column c appears in exactly 4 stored blocks, whose output blocks are c, c xor 1, c xor (16) and c xor (32); the stored blocks on one index of wloop are exactly those of its 16 input block columns, in an order drawn afresh. `block_cols`: the input block column of each stored block, as described for block_rows; the stored blocks on one index of wloop have input columns within that index's range of 16 columns.
All inputs are finite; a program needn't handle non-finite values.
Results may differ from a plain program's by a relative error of at most 0.0039.
Values may be sent and summed in bfloat16 or wider, within the bound.
A program may use at most 128 MiB of HBM per device.

v0:
```python
import jax
import jax.numpy as jnp
from jax import lax
from jax.sharding import PartitionSpec as P

WIDTH = 16384
BLOCK = 256


def swapped(block, axis, apart):
    count = lax.axis_size(axis)
    route = []
    for low in range(count):
        high = low | 1 << apart
        if high != low and high < count:
            route += [(low, high), (high, low)]
    return lax.ppermute(block, axis, route)


def flip_pairs(values):
    rows_here, share, width = values.shape
    return values.reshape(rows_here, share // 2, 2, width)[:, :, ::-1].reshape(
        rows_here, share, width
    )


def apply_blocks(inputs, weights):
    return jnp.einsum("rjk,ojk->rjo", inputs, weights, preferred_element_type=jnp.float32)


def weight_grad(grads, inputs):
    return jnp.einsum("rjo,rjk->ojk", grads, inputs, preferred_element_type=jnp.float32)


def body(features, cotangent, block_weights, block_rows, block_cols, lowrank_in, lowrank_out):
    rows_here = features.shape[0]
    share = features.shape[1] // BLOCK
    count = WIDTH // BLOCK
    local_cols = block_cols % share
    stride_of = jnp.bitwise_xor(block_rows, block_cols)
    stride_table = jnp.array([0, 1, count // 4, count // 2], jnp.int32)
    positions = jnp.arange(share, dtype=jnp.int32)
    select = (local_cols[None, None, :] == positions[None, :, None]) & (
        stride_of[None, None, :] == stride_table[:, None, None]
    )
    by_stride = jnp.einsum(
        "sjl,lab->sajb",
        select.astype(jnp.bfloat16),
        block_weights,
        preferred_element_type=jnp.float32,
    ).astype(jnp.bfloat16)
    blocked = features.reshape(rows_here, share, BLOCK)
    grads_blocked = cotangent.reshape(rows_here, share, BLOCK)
    dims = (((1,), (1,)), ((), ()))
    partial_code = lax.dot_general(features, lowrank_in, dims, preferred_element_type=jnp.float32)
    partial_back = lax.dot_general(cotangent, lowrank_out, dims, preferred_element_type=jnp.float32)
    codes, backs = lax.psum((partial_code, partial_back), "wloop")
    codes = codes.astype(jnp.bfloat16)
    backs = backs.astype(jnp.bfloat16)
    total = apply_blocks(blocked, by_stride[0]) + flip_pairs(apply_blocks(blocked, by_stride[1]))
    grad_list = [
        weight_grad(grads_blocked, blocked),
        weight_grad(flip_pairs(grads_blocked), blocked),
    ]
    top_bit = lax.axis_size("wloop").bit_length() - 1
    far_bits = (top_bit - 2, top_bit - 1)
    for index in (2, 3):
        outgoing = apply_blocks(blocked, by_stride[index]).reshape(rows_here, share * BLOCK)
        arrived = swapped(outgoing, "wloop", far_bits[index - 2])
        total = total + arrived.reshape(rows_here, share, BLOCK)
        their_grads = swapped(cotangent, "wloop", far_bits[index - 2])
        grad_list.append(weight_grad(their_grads.reshape(rows_here, share, BLOCK), blocked))
    low_part = jnp.dot(codes, lowrank_out, preferred_element_type=jnp.float32)
    mixed = (total.reshape(rows_here, share * BLOCK) + low_part).astype(jnp.bfloat16)
    grad_blocks = jnp.stack(grad_list, axis=1)
    cols_dims = (((0,), (0,)), ((), ()))
    grad_in_term = lax.dot_general(backs, features, cols_dims, preferred_element_type=jnp.float32)
    grad_out_term = lax.dot_general(codes, cotangent, cols_dims, preferred_element_type=jnp.float32)
    block_share, grad_in, grad_out = (
        lax.psum_scatter(grad_blocks, "items", scatter_dimension=0, tiled=True),
        lax.psum_scatter(grad_in_term, "items", scatter_dimension=0, tiled=True),
        lax.psum_scatter(grad_out_term, "items", scatter_dimension=0, tiled=True),
    )
    block_grads = jnp.einsum(
        "sjl,asjb->alb", select.astype(jnp.float32), block_share, precision=lax.Precision.HIGHEST
    )
    return (mixed, block_grads, grad_in, grad_out)


def solution(mesh):
    return jax.shard_map(
        body,
        mesh=mesh,
        in_specs=(
            P(("groups", "items"), "wloop"),
            P(("groups", "items"), "wloop"),
            P("wloop", None, None),
            P("wloop"),
            P("wloop"),
            P(None, "wloop"),
            P(None, "wloop"),
        ),
        out_specs=(
            P(("groups", "items"), "wloop"),
            P(("groups", "items"), "wloop", None),
            P(("groups", "items"), "wloop"),
            P(("groups", "items"), "wloop"),
        ),
        check_vma=False,
    )
```

profile of v0, /device:TPU:0, one launch (start us, length us, event | category | flops | bytes accessed | tf_op | source)
XLA Modules:
  0.0 398.0 jit_solution(13207586459639743358)
XLA Ops:
  7.2 0.0 copy-start
  7.2 0.0 copy-start.1
  7.2 0.0 reduce-scatter.4.cloned.1.call-start
  7.2 4.2 %copy.64 = bf16[256,4096]{0,1:T(8,128)(2,1)} copy(bf16[256,4096]{1,0:T(8,128)(2,1)} %param.9) | data formatting | bytes 4194304 | tf_op args[1]
  11.5 4.0 %collective-permute-start.3 = (bf16[256,4096]{0,1:T(8,128)(2,1)}, bf16[256,4096]{0,1:T(8,128)(2,1)}, u32[]{:S(2)}, u32[]{:S(2)}) collective-permute-start(bf16[256,4096]{0,1:T(8,128)(2,1)} %copy.64), channel_id=1, source_target_pairs={{0,8},{8,0},{4,12},{12,4},{1,9},{9,1},{5,13},{13,5},{2,10},{10,2},... | collective-permute-start | bytes 6291464 | tf_op jit(solution)/shard_map/ppermute | solution.py:17
  15.5 1.6 collective-permute-start.2
  17.1 0.0 copy-done.1
  17.1 2.7 reshape_reshape.3
  19.8 3.3 copy.75
  23.1 19.7 %rev.7 = bf16[256,8,2,256]{3,2,1,0:T(2,128)(2,1)} reverse(bf16[256,8,2,256]{3,2,1,0:T(2,128)(2,1)} %reshape_reshape.3), dimensions={2} | reverse | bytes 4194304 | tf_op jit(solution)/shard_map/rev | solution.py:22
  42.8 2.3 copy.62
  45.1 0.0 copy-start.2
  45.1 0.7 convolution_bitcast_fusion.3
  45.8 0.9 copy-done.2
  46.7 0.7 convolution_bitcast_fusion.4
  47.4 59.1 %collective-permute-done.3 = bf16[256,4096]{0,1:T(8,128)(2,1)} collective-permute-done((bf16[256,4096]{0,1:T(8,128)(2,1)}, bf16[256,4096]{0,1:T(8,128)(2,1)}, u32[]{:S(2)}, u32[]{:S(2)}) %collective-permute-start.3) | collective-permute-done | bytes 2097184 | tf_op jit(solution)/shard_map/ppermute | solution.py:17
  106.5 2.3 convolution_bitcast_fusion.1
  108.8 0.0 collective-permute-done.2
  108.8 2.3 convolution_bitcast_fusion.2
  111.2 6.4 %pad_maximum_fusion = f32[256,4,16,256]{0,3,2,1:T(8,128)} fusion(f32[256,1,16,256]{0,3,2,1:T(8,128)S(1)} %convolution_bitcast_fusion.1, f32[256,1,16,256]{0,3,2,1:T(8,128)S(1)} %convolution_bitcast_fusion.2, f32[256,1,16,256]{0,3,2,1:T(8,128)S(1)} %convolution_bitcast_fusion.3, f32[256,1,16,256]{0,3,2,1:T(8,128)S(1)} %convolution_bitcast_fusion.4), kind=kLoop, calls=%fused_computation | loop fusion | flops 12582912 | bytes 33554432 | tf_op jit(solution)/shard_map/stack | solution.py:75
  117.5 19.9 %copy.70 = f32[256,4,16,256]{3,2,1,0:T(8,128)} copy(f32[256,4,16,256]{0,3,2,1:T(8,128)} %pad_maximum_fusion) | data formatting | bytes 33554432 | tf_op jit(solution)/shard_map/stack | solution.py:75
  137.4 0.0 reduce-scatter.4.cloned.1.call-update
  137.4 0.0 reduce-scatter.8.cloned.1.call-start
  137.5 0.0 copy-start.3
  137.5 2.7 fusion.28
  140.2 0.0 copy-done
  140.2 0.0 copy-done.3
  140.2 0.7 fusion.29
  140.9 24.6 %all-reduce.2 = (bf16[256,128]{1,0:T(8,128)(2,1)S(1)}, bf16[256,128]{1,0:T(8,128)(2,1)S(1)}) all-reduce(f32[256,128]{1,0:T(8,128)S(1)} %fusion.28, f32[256,128]{1,0:T(8,128)S(1)} %fusion.29), channel_id=1, replica_groups=mesh['groups'=2,'wloop'=4,'items'=4] {'wloop'}, use_global_device_ids=true, to_apply=%region_0.1 | all-reduce | flops 65536 | bytes 393216 | tf_op jit(solution)/shard_map/psum | solution.py:57
  165.6 3.4 fusion.31
  169.0 0.0 copy-start.7
  169.0 0.0 copy-start.8
  169.0 0.0 copy-start.9
  169.0 0.0 reduce-scatter.8.cloned.1.call-update
  169.1 0.2 reduce-scatter.6.cloned.1.call-start
  169.3 0.4 copy-done.7
  169.7 0.0 copy-done.8
  169.7 0.0 copy-done.9
  169.7 0.1 broadcast_compare_fusion
  169.8 10.8 %convert_bitcast_fusion = bf16[4,256,16,256]{3,2,1,0:T(8,128)(2,1)S(1)} fusion(bf16[64,256,256]{2,1,0:T(8,128)(2,1)} %param.10, pred[4,64]{1,0:T(4,128)(4,1)S(1)} %broadcast_compare_fusion, pred[16,64]{1,0:T(8,128)(4,1)S(1)} %iota_compare_fusion), kind=kOutput, calls=%fused_computation.4 | convolution fusion | flops 541069312 | bytes 16778496 | tf_op jit(solution)/shard_map/sjl,lab->sajb/dot_general | solution.py:46
  180.6 2.5 slice_bitcast_fusion.3
  183.1 2.8 fusion.11
  185.9 0.0 collective-permute-start
  185.9 0.0 copy-start.4
  185.9 2.9 fusion.9
  188.8 0.3 collective-permute-start.1
  189.1 0.0 copy-done.4
  189.1 1.8 fusion.30
  190.9 0.0 reduce-scatter.6.cloned.1.call-update
  190.9 4.7 %fusion.13 = f32[16,256,256]{2,1,0:T(8,128)} fusion(bf16[256,16,256]{0,2,1:T(8,128)(2,1)S(1)} %bitcast.99, bf16[256,16,256]{2,1,0:T(8,128)(2,1)} %get-tuple-element.9), kind=kOutput, calls=%fused_computation.24 | convolution fusion | flops 536870912 | bytes 8388608 | tf_op jit(solution)/shard_map/rjk,ojk->rjo/dot_general | solution.py:28
  195.6 4.6 %rev.6 = f32[256,8,2,256]{0,3,2,1:T(8,128)} reverse(f32[256,8,2,256]{0,3,2,1:T(8,128)} %bitcast.103), dimensions={2} | reverse | bytes 8388608 | tf_op jit(solution)/shard_map/rev | solution.py:22
  200.2 0.0 copy-start.6
  200.2 2.8 fusion.32
  203.0 0.0 copy-done.6
  203.0 0.0 copy-start.5
  203.0 0.9 fusion.15
  203.9 156.4 %collective-permute-done = f32[256,4096]{0,1:T(8,128)} collective-permute-done((f32[256,4096]{0,1:T(8,128)}, f32[256,4096]{0,1:T(8,128)}, u32[]{:S(2)}, u32[]{:S(2)}) %collective-permute-start) | collective-permute-done | bytes 4194336 | tf_op jit(solution)/shard_map/ppermute | solution.py:17
  360.3 7.2 %collective-permute-done.1 = f32[256,4096]{0,1:T(8,128)} collective-permute-done((f32[256,4096]{0,1:T(8,128)}, f32[256,4096]{0,1:T(8,128)}, u32[]{:S(2)}, u32[]{:S(2)}) %collective-permute-start.1) | collective-permute-done | bytes 4194336 | tf_op jit(solution)/shard_map/ppermute | solution.py:17
  367.5 0.0 copy-done.5
  367.5 6.6 %fusion.6 = f32[256,16,256]{0,2,1:T(8,128)} fusion(f32[256,16,256]{0,2,1:T(8,128)} %bitcast.17, f32[256,16,256]{0,2,1:T(8,128)} %bitcast.13, f32[256,8,2,256]{0,3,2,1:T(8,128)S(1)} %copy-done.5, f32[16,256,256]{2,1,0:T(8,128)S(1)} %fusion.15), kind=kLoop, calls=%fused_computation.7 | loop fusion | flops 3145728 | bytes 20971520 | tf_op jit(solution)/shard_map/add | solution.py:70
  374.1 5.7 %copy.59 = f32[256,4096]{1,0:T(8,128)} copy(f32[256,4096]{0,1:T(8,128)} %bitcast.102) | data formatting | bytes 8388608 | tf_op jit(solution)/shard_map/reshape | solution.py:74
  379.8 5.3 %add_convert_fusion = bf16[256,4096]{1,0:T(8,128)(2,1)} fusion(f32[256,4096]{1,0:T(8,128)} %copy.59, f32[256,4096]{1,0:T(8,128)} %fusion.32), kind=kLoop, calls=%fused_computation.8 | loop fusion | flops 2097152 | bytes 10485760 | tf_op jit(solution)/shard_map/convert_element_type | solution.py:74
  385.1 0.0 reduce-scatter.4.cloned.1.call-done
  385.1 6.3 %convolution_bitcast_fusion = f32[64,64,256]{2,1,0:T(8,128)} fusion(f32[64,4,16,256]{3,2,1,0:T(8,128)} %reduce-scatter.4.cloned.1.call-done, pred[4,64]{1,0:T(4,128)(4,1)S(1)} %broadcast_compare_fusion, pred[16,64]{1,0:T(8,128)(4,1)S(1)} %iota_compare_fusion), kind=kOutput, calls=%fused_computation.9 | convolution fusion | flops 805310464 | bytes 8389888 | tf_op jit(solution)/shard_map/sjl,asjb->alb/dot_general | solution.py:84
  (4 shorter events, 0.0 us)
Async XLA Ops:
  7.2 133.1 %copy-start = (bf16[128,4096]{1,0:T(8,128)(2,1)S(1)}, bf16[128,4096]{1,0:T(8,128)(2,1)}, u32[]{:S(2)}) copy-start(bf16[128,4096]{1,0:T(8,128)(2,1)} %param.14) | copy-start | bytes 3145732
  7.2 9.9 %copy-start.1 = (bf16[256,4096]{1,0:T(8,128)(2,1)S(1)}, bf16[256,4096]{1,0:T(8,128)(2,1)}, u32[]{:S(2)}) copy-start(bf16[256,4096]{1,0:T(8,128)(2,1)} %param.9) | copy-start | bytes 6291460
  7.2 377.9 %reduce-scatter.4.cloned.1.call-start = ((), (), s32[]{:S(2)}) async-start(), calls=%async_computation.3 | async-start | bytes 20971520 | tf_op jit(solution)/shard_map/reduce_scatter | solution.py:80
  11.5 95.0 %collective-permute-start.3 = (bf16[256,4096]{0,1:T(8,128)(2,1)}, bf16[256,4096]{0,1:T(8,128)(2,1)}, u32[]{:S(2)}, u32[]{:S(2)}) collective-permute-start(bf16[256,4096]{0,1:T(8,128)(2,1)} %copy.64), channel_id=1, source_target_pairs={{0,8},{8,0},{4,12},{12,4},{1,9},{9,1},{5,13},{13,5},{2,10},{10,2},... | collective-permute-start | bytes 6291464 | tf_op jit(solution)/shard_map/ppermute | solution.py:17
  15.5 93.3 %collective-permute-start.2 = (bf16[256,4096]{0,1:T(8,128)(2,1)}, bf16[256,4096]{0,1:T(8,128)(2,1)}, u32[]{:S(2)}, u32[]{:S(2)}) collective-permute-start(bf16[256,4096]{0,1:T(8,128)(2,1)} %copy.64), channel_id=1, source_target_pairs={{0,4},{4,0},{8,12},{12,8},{1,5},{5,1},{9,13},{13,9},{2,6},{6,2},{1... | collective-permute-start | bytes 6291464 | tf_op jit(solution)/shard_map/ppermute | solution.py:17
  45.1 1.6 copy-start.2
  137.4 254.0 %reduce-scatter.8.cloned.1.call-start = ((), (), s32[]{:S(2)}) async-start(), calls=%async_computation.5 | async-start | bytes 2621440 | tf_op jit(solution)/shard_map/reduce_scatter | solution.py:82
  137.5 2.7 copy-start.3
  169.0 0.7 copy-start.7
  169.0 0.7 copy-start.8
  169.0 0.7 copy-start.9
  169.1 222.4 %reduce-scatter.6.cloned.1.call-start = ((), (), s32[]{:S(2)}) async-start(), calls=%async_computation.4 | async-start | bytes 2621440 | tf_op jit(solution)/shard_map/reduce_scatter | solution.py:81
  185.9 174.4 %collective-permute-start = (f32[256,4096]{0,1:T(8,128)}, f32[256,4096]{0,1:T(8,128)}, u32[]{:S(2)}, u32[]{:S(2)}) collective-permute-start(f32[256,4096]{0,1:T(8,128)} %bitcast.12), channel_id=1, source_target_pairs={{0,4},{4,0},{8,12},{12,8},{1,5},{5,1},{9,13},{13,9},{2,6},{6,2},{1... | collective-permute-start | bytes 12582920 | tf_op jit(solution)/shard_map/ppermute | solution.py:17
  185.9 3.2 copy-start.4
  188.8 178.7 %collective-permute-start.1 = (f32[256,4096]{0,1:T(8,128)}, f32[256,4096]{0,1:T(8,128)}, u32[]{:S(2)}, u32[]{:S(2)}) collective-permute-start(f32[256,4096]{0,1:T(8,128)} %bitcast.16), channel_id=1, source_target_pairs={{0,8},{8,0},{4,12},{12,4},{1,9},{9,1},{5,13},{13,5},{2,10},{10,2},... | collective-permute-start | bytes 12582920 | tf_op jit(solution)/shard_map/ppermute | solution.py:17
  200.2 2.8 copy-start.6
  203.0 164.5 %copy-start.5 = (f32[256,8,2,256]{0,3,2,1:T(8,128)S(1)}, f32[256,8,2,256]{0,3,2,1:T(8,128)}, u32[]{:S(2)}) copy-start(f32[256,8,2,256]{0,3,2,1:T(8,128)} %rev.6) | copy-start | bytes 12582916
Sparse Core Ops, SparseCore 0:
  137.6 127.2 reduce-scatter.3
  268.1 31.4 reduce-scatter.7
  302.6 31.3 reduce-scatter.5
where the time goes:
time: 400 us; the launch traced here: 398 us
  waiting for transfers between devices  223 us (56%)
  local copies, waits for them, and re-layouts  66.2 us (17%)
  matrix products  46 us (12%)
  blocking collectives  24.6 us (6%)
  other arithmetic  18.3 us (5%)
  between operations  13.9 us (3%)
  starting transfers between devices  6.19 us (2%)
    ppermute x4, waiting for transfers between devices, swapped(): return lax.ppermute(block, axis, route)  223 us
    rev x3, local copies, waits for them, and re-layouts, flip_pairs(): values.reshape(rows_here, share // 2, 2, width)[:, :, ::-1]  26.6 us
    psum x1, blocking collectives, body(): codes, backs = lax.psum((partial_code, partial_back), 'wloop')  24.6 us
    another operation x1, local copies, waits for them, and re-layouts, body(): grad_blocks = jnp.stack(grad_list, axis=1)  19.9 us
    dot_general x4, matrix products, apply_blocks(): jnp.einsum('rjk,ojk->rjo', inputs, weights, preferred_element_type=jnp.fl...  11.4 us
    dot_general x1, matrix products, body(): jnp.einsum('sjl,lab->sajb', select.astype(jnp.bfloat16), block_weights, p...  10.8 us
  transfers between devices with their start and end apart: 7, of which 3 were waited for; matrix products, arithmetic and copies ran while one was open for 24% of the time, Pallas kernels for 0%

commit v1 on v0

v1 whole, which is shorter than its diff:
```python
import functools

import jax
import jax.numpy as jnp
from jax import lax
from jax.experimental import pallas as pl
from jax.experimental.pallas import tpu as pltpu
from jax.sharding import PartitionSpec as P

WIDTH = 16384
BLOCK = 256
LOWRANK = 128
F32 = jnp.float32
BF16 = jnp.bfloat16
NT = (((1,), (1,)), ((), ()))
TN = (((0,), (0,)), ((), ()))


def dot(a, b, dims=(((1,), (0,)), ((), ()))):
    return lax.dot_general(a, b, dims, preferred_element_type=F32)


def cost(flops, bytes_accessed):
    return pl.CostEstimate(flops=int(flops), bytes_accessed=int(bytes_accessed), transcendentals=0)


def params():
    return pltpu.CompilerParams(vmem_limit_bytes=40 << 20)


def swapped(block, axis, apart):
    count = lax.axis_size(axis)
    route = []
    for low in range(count):
        high = low | 1 << apart
        if high != low and high < count:
            route += [(low, high), (high, low)]
    return lax.ppermute(block, axis, route)


def column(rows):
    return pl.BlockSpec((rows, BLOCK), lambda j, *_: (0, j))


def paired(rows):
    return pl.BlockSpec((rows, BLOCK), lambda j, *_: (0, j + 1 - 2 * (j % 2)))


def stored(stride, flip=False):
    def place(j, table):
        if flip:
            j = j + 1 - 2 * (j % 2)
        return (table[stride, j], 0, 0)

    return pl.BlockSpec((1, BLOCK, BLOCK), place)


def far_kernel(table, x, wa, wb, oa, ob):
    oa[...] = dot(x[...], wa[0], NT).astype(BF16)
    ob[...] = dot(x[...], wb[0], NT).astype(BF16)


def far_partials(table, features, weights):
    rows, width = features.shape
    return pl.pallas_call(
        far_kernel,
        out_shape=[jax.ShapeDtypeStruct((rows, width), BF16)] * 2,
        grid_spec=pltpu.PrefetchScalarGridSpec(
            num_scalar_prefetch=1,
            grid=(width // BLOCK,),
            in_specs=[column(rows), stored(2), stored(3)],
            out_specs=[column(rows)] * 2,
        ),
        compiler_params=params(),
        cost_estimate=cost(4 * rows * width * BLOCK, 6 * rows * width + 4 * width * BLOCK),
    )(table, features, weights, weights)


def near_kernel(table, x, y, wa, wb, c, low, o):
    o[...] = dot(x[...], wa[0], NT) + dot(y[...], wb[0], NT) + dot(c[...], low[...])


def near_total(table, features, weights, codes, lowrank_out):
    rows, width = features.shape
    return pl.pallas_call(
        near_kernel,
        out_shape=jax.ShapeDtypeStruct((rows, width), F32),
        grid_spec=pltpu.PrefetchScalarGridSpec(
            num_scalar_prefetch=1,
            grid=(width // BLOCK,),
            in_specs=[
                column(rows),
                paired(rows),
                stored(0),
                stored(1, True),
                pl.BlockSpec((rows, LOWRANK), lambda j, *_: (0, 0)),
                column(LOWRANK),
            ],
            out_specs=column(rows),
        ),
        compiler_params=params(),
        cost_estimate=cost(4 * rows * width * BLOCK, 8 * rows * width + 4 * width * BLOCK),
    )(table, features, features, weights, weights, codes, lowrank_out)


def near_grad_kernel(n, x, g, h, o):
    part = BLOCK // n
    o[:, 0, 0] = dot(g[...], x[...], TN).reshape(n, part, BLOCK)
    o[:, 0, 1] = dot(h[...], x[...], TN).reshape(n, part, BLOCK)


def near_grads(n, features, cotangent):
    rows, width = features.shape
    share = width // BLOCK
    return pl.pallas_call(
        functools.partial(near_grad_kernel, n),
        grid=(share,),
        out_shape=jax.ShapeDtypeStruct((n, share, 2, BLOCK // n, BLOCK), F32),
        in_specs=[column(rows), column(rows), paired(rows)],
        out_specs=pl.BlockSpec((n, 1, 2, BLOCK // n, BLOCK), lambda j: (0, j, 0, 0, 0)),
        compiler_params=params(),
        cost_estimate=cost(4 * rows * width * BLOCK, 6 * rows * width + 8 * width * BLOCK),
    )(features, cotangent, cotangent)


def far_grad_kernel(n, x, g, ga, gb, codes, backs, o):
    part = BLOCK // n
    half = part // 2
    o[:, 0, 0] = dot(ga[...], x[...], TN).reshape(n, part, BLOCK)
    o[:, 0, 1] = dot(gb[...], x[...], TN).reshape(n, part, BLOCK)
    o[:, 0, 2, :half] = dot(backs[...], x[...], TN).reshape(n, half, BLOCK)
    o[:, 0, 2, half:] = dot(codes[...], g[...], TN).reshape(n, half, BLOCK)


def far_grads(n, features, cotangent, from_a, from_b, codes, backs):
    rows, width = features.shape
    share = width // BLOCK
    whole = pl.BlockSpec((rows, LOWRANK), lambda j: (0, 0))
    return pl.pallas_call(
        functools.partial(far_grad_kernel, n),
        grid=(share,),
        out_shape=jax.ShapeDtypeStruct((n, share, 3, BLOCK // n, BLOCK), F32),
        in_specs=[column(rows)] * 4 + [whole] * 2,
        out_specs=pl.BlockSpec((n, 1, 3, BLOCK // n, BLOCK), lambda j: (0, j, 0, 0, 0)),
        compiler_params=params(),
        cost_estimate=cost(6 * rows * width * BLOCK, 8 * rows * width + 12 * width * BLOCK),
    )(features, cotangent, from_a, from_b, codes, backs)


def place_kernel(share, table, near, far, blocks, grad_in, grad_out):
    half = grad_in.shape[0]
    for j in range(share):
        for s in range(4):
            value = near[j, s] if s < 2 else far[j, s - 2]
            blocks[:, pl.ds(table[s, j], 1), :] = value[:, None, :]
        grad_in[:, j * BLOCK : (j + 1) * BLOCK] = far[j, 2, :half]
        grad_out[:, j * BLOCK : (j + 1) * BLOCK] = far[j, 2, half:]


def place(table, near, far):
    share, _, part, _ = near.shape
    vmem = pl.BlockSpec(memory_space=pltpu.VMEM)
    return pl.pallas_call(
        functools.partial(place_kernel, share),
        out_shape=[
            jax.ShapeDtypeStruct((part, 4 * share, BLOCK), F32),
            jax.ShapeDtypeStruct((part // 2, share * BLOCK), F32),
            jax.ShapeDtypeStruct((part // 2, share * BLOCK), F32),
        ],
        in_specs=[pl.BlockSpec(memory_space=pltpu.SMEM), vmem, vmem],
        out_specs=[vmem] * 3,
        compiler_params=params(),
        cost_estimate=cost(0, 40 * share * part * BLOCK),
    )(table, near, far)


def body(features, cotangent, block_weights, block_rows, block_cols, lowrank_in, lowrank_out):
    share = features.shape[1] // BLOCK
    count = WIDTH // BLOCK
    items = lax.axis_size("items")
    top_bit = lax.axis_size("wloop").bit_length() - 1
    local_cols = block_cols % share
    stride_of = jnp.bitwise_xor(block_rows, block_cols)
    strides = jnp.array([0, 1, count // 4, count // 2], jnp.int32)
    positions = jnp.arange(share, dtype=jnp.int32)
    select = (local_cols[None, None, :] == positions[None, :, None]) & (
        stride_of[None, None, :] == strides[:, None, None]
    )
    numbers = jnp.arange(block_rows.shape[0], dtype=jnp.int32)
    table = jnp.sum(jnp.where(select, numbers[None, None, :], 0), axis=2).astype(jnp.int32)

    from_a = swapped(cotangent, "wloop", top_bit - 2)
    from_b = swapped(cotangent, "wloop", top_bit - 1)
    near = near_grads(items, features, cotangent)
    partial_code = dot(features, lowrank_in, NT)
    partial_back = dot(cotangent, lowrank_out, NT)
    codes, backs = lax.psum((partial_code, partial_back), "wloop")
    codes = codes.astype(BF16)
    backs = backs.astype(BF16)
    near_share = lax.psum_scatter(near, "items", scatter_dimension=0, tiled=True)[0]
    to_a, to_b = far_partials(table, features, block_weights)
    to_a, to_b, from_a, from_b, codes, backs = lax.optimization_barrier(
        (to_a, to_b, from_a, from_b, codes, backs)
    )
    got_a = swapped(to_a, "wloop", top_bit - 2)
    got_b = swapped(to_b, "wloop", top_bit - 1)
    far = far_grads(items, features, cotangent, from_a, from_b, codes, backs)
    far_share = lax.psum_scatter(far, "items", scatter_dimension=0, tiled=True)[0]
    total = near_total(table, features, block_weights, codes, lowrank_out)
    block_grads, grad_in, grad_out = place(table, near_share, far_share)
    mixed = (total + got_a.astype(F32) + got_b.astype(F32)).astype(BF16)
    return (mixed, block_grads, grad_in, grad_out)


def solution(mesh):
    return jax.shard_map(
        body,
        mesh=mesh,
        in_specs=(
            P(("groups", "items"), "wloop"),
            P(("groups", "items"), "wloop"),
            P("wloop", None, None),
            P("wloop"),
            P("wloop"),
            P(None, "wloop"),
            P(None, "wloop"),
        ),
        out_specs=(
            P(("groups", "items"), "wloop"),
            P(("groups", "items"), "wloop", None),
            P(("groups", "items"), "wloop"),
            P(("groups", "items"), "wloop"),
        ),
        check_vma=False,
    )
```

time: 400 us -> 264 us (0.66)
  waiting for transfers between devices: 223 us -> 80.4 us
  blocking collectives: 24.6 us -> 91.3 us
  local copies, waits for them, and re-layouts: 66.2 us -> 15.6 us
  Pallas kernels: 0 us -> 50.1 us
  matrix products: 46 us -> 1.41 us
  other arithmetic: 18.3 us -> 2.57 us
    ppermute x4, waiting for transfers between devices: 223 us -> 73.9 us  [swapped(): return lax.ppermute(block, axis, route)]
    psum x1, blocking collectives: 24.6 us -> 91.3 us  [body(): codes, backs = lax.psum((partial_code, partial_back), 'wloop')]
    pallas_call x0 -> x5, Pallas kernels: none -> 50.1 us  [the longest x1 14.2 us: far_grads(): pl.pallas_call(functools.partial(far_grad_kernel, n), grid=(share,), out_...]
    dot_general x15 -> x2, matrix products: 46 us -> 1.41 us  [dot(): return lax.dot_general(a, b, dims, preferred_element_type=F32)]
    rev x3 -> x0, local copies, waits for them, and re-layouts: 26.6 us -> none  [flip_pairs(): values.reshape(rows_here, share // 2, 2, width)[:, :, ::-1]]
    another operation x2 -> x0, local copies, waits for them, and re-layouts: 22.6 us -> none  [the longest x1 19.9 us: body(): grad_blocks = jnp.stack(grad_list, axis=1)]
    unnamed x21 -> x32, local copies, waits for them, and re-layouts: 5.54 us -> 15.6 us
    reshape x2 -> x0, local copies, waits for them, and re-layouts: 8.95 us -> none  [the longest x1 5.68 us: body(): total.reshape(rows_here, share * BLOCK) + low_part]
  transfers between devices with their start and end apart: 7 -> 6, of which waited for: 3 -> 3; matrix products, arithmetic and copies ran while one was open for 24% -> 2% of each run, Pallas kernels for 0% -> 15%
where the time goes in v1:
time: 264 us; the launch traced here: 263 us
  blocking collectives  91.3 us (35%)
  waiting for transfers between devices  80.4 us (30%)
  Pallas kernels  50.1 us (19%)
  local copies, waits for them, and re-layouts  15.6 us (6%)
  between operations  14.2 us (5%)
  starting transfers between devices  6.84 us (3%)
    psum x1, blocking collectives, body(): codes, backs = lax.psum((partial_code, partial_back), 'wloop')  91.3 us
    ppermute x4, waiting for transfers between devices, swapped(): return lax.ppermute(block, axis, route)  73.9 us
    unnamed x32, local copies, waits for them, and re-layouts  15.6 us
    pallas_call x1, Pallas kernels, far_grads(): pl.pallas_call(functools.partial(far_grad_kernel, n), grid=(share,), out_...  14.2 us
    pallas_call x1, Pallas kernels, near_total(): pl.pallas_call(near_kernel, out_shape=jax.ShapeDtypeStruct((rows, width),...  12.7 us
    pallas_call x1, Pallas kernels, far_partials(): pl.pallas_call(far_kernel, out_shape=[jax.ShapeDtypeStruct((rows, width),...  12.1 us
    ppermute x4, starting transfers between devices, swapped(): return lax.ppermute(block, axis, route)  6.76 us
    reduce_scatter x1, waiting for transfers between devices, body(): lax.psum_scatter(far, 'items', scatter_dimension=0, tiled=True)[0]  6.46 us
  transfers between devices with their start and end apart: 6, of which 3 were waited for; matrix products, arithmetic and copies ran while one was open for 2% of the time, Pallas kernels for 15%

profile of v1, /device:TPU:0, one launch (start us, length us, event | category | flops | bytes accessed | tf_op | source)
XLA Modules:
  0.0 262.5 jit_solution(14255100619794826726)
XLA Ops:
  7.2 0.0 copy-start
  7.2 0.0 reduce-scatter.3.cloned.1.call-start
  7.2 0.0 copy-start.1
  7.2 1.7 copy-done.1
  8.9 0.0 copy-start.3
  8.9 1.6 copy-done.3
  10.5 5.9 %shard_map.113 = f32[4,16,2,64,256]{4,3,2,1,0:T(8,128)S(1)} custom-call(bf16[256,4096]{1,0:T(8,128)(2,1)S(1)} %copy-done.1, bf16[256,4096]{1,0:T(8,128)(2,1)S(1)} %copy-done.3, bf16[256,4096]{1,0:T(8,128)(2,1)S(1)} %copy-done.3), custom_call_target="tpu_custom_call" | custom-call | flops 1073741824 | bytes 14680064 | tf_op jit(solution)/shard_map/pallas_call | solution.py:115
  16.4 0.0 copy-start.6
  16.4 3.4 %copy-done.6 = f32[4,16,2,64,256]{4,3,2,1,0:T(8,128)} copy-done((f32[4,16,2,64,256]{4,3,2,1,0:T(8,128)}, f32[4,16,2,64,256]{4,3,2,1,0:T(8,128)S(1)}, u32[]{:S(2)}) %copy-start.6) | copy-done | bytes 8388632
  19.8 0.0 copy-start.2
  19.8 0.0 reduce-scatter.3.cloned.1.call-update
  19.8 0.0 reduce-scatter.5.cloned.1.call-start
  19.9 0.0 copy-start.4
  19.9 0.0 copy-start.7
  19.9 4.1 %collective-permute-start.1 = (bf16[256,4096]{1,0:T(8,128)(2,1)}, bf16[256,4096]{1,0:T(8,128)(2,1)}, u32[]{:S(2)}, u32[]{:S(2)}) collective-permute-start(bf16[256,4096]{1,0:T(8,128)(2,1)} %g.3), channel_id=1, source_target_pairs={{0,8},{8,0},{4,12},{12,4},{1,9},{9,1},{5,13},{13,5},{2,10},{10,2},... | collective-permute-start | bytes 6291464 | tf_op jit(solution)/shard_map/ppermute | solution.py:38
  24.0 1.6 collective-permute-start
  25.6 0.0 copy-done
  25.6 0.0 copy-done.2
  25.6 0.7 fusion.1
  26.3 0.0 copy-done.4
  26.3 0.0 copy-done.7
  26.3 0.0 copy-start.13
  26.3 0.0 copy-start.14
  26.3 0.0 copy-start.15
  26.3 0.7 fusion.2
  27.0 0.0 copy-done.13
  27.1 0.0 copy-done.14
  27.1 0.0 copy-done.15
  27.1 0.1 broadcast_compare_fusion
  27.2 0.2 select_reduce_fusion.table
  27.3 12.1 %shard_map.111 = (bf16[256,4096]{1,0:T(8,128)(2,1)S(1)}, bf16[256,4096]{1,0:T(8,128)(2,1)S(1)}) custom-call(s32[4,16]{1,0:T(4,128)S(1)} %select_reduce_fusion.table, bf16[256,4096]{1,0:T(8,128)(2,1)S(1)} %copy-done.2, bf16[64,256,256]{2,1,0:T(8,128)(2,1)} %wb.3, bf16[64,256,256]{2,1,0:T(8,128)(2,1)} %wb.3), custom_call_target="tpu_custom_call" | custom-call | flops 1073741824 | bytes 10485760 | tf_op jit(solution)/shard_map/pallas_call | solution.py:65
  39.5 0.0 copy-start.11
  39.5 1.3 copy-done.11
  40.8 0.0 copy-start.12
  40.8 1.3 copy-done.12
  42.1 91.3 %all-reduce.2 = (bf16[256,128]{1,0:T(8,128)(2,1)S(1)}, bf16[256,128]{1,0:T(8,128)(2,1)S(1)}) all-reduce(f32[256,128]{1,0:T(8,128)S(1)} %fusion.1, f32[256,128]{1,0:T(8,128)S(1)} %fusion.2), channel_id=1, replica_groups=mesh['groups'=2,'wloop'=4,'items'=4] {'wloop'}, use_global_device_ids=true, to_apply=%region_1.2 | all-reduce | flops 65536 | bytes 393216 | tf_op jit(solution)/shard_map/psum | solution.py:197
  133.4 0.0 collective-permute-done.1.gb
  133.4 0.0 collective-permute-done.ga
  133.4 0.0 copy-start.5
  133.4 1.6 copy-done.5
  135.0 14.2 %shard_map.114 = f32[4,16,3,64,256]{4,3,2,1,0:T(8,128)} custom-call(bf16[256,4096]{1,0:T(8,128)(2,1)S(1)} %copy-done.2, bf16[256,4096]{1,0:T(8,128)(2,1)S(1)} %copy-done.5, bf16[256,4096]{1,0:T(8,128)(2,1)} %collective-permute-done.ga, bf16[256,4096]{1,0:T(8,128)(2,1)} %collective-permute-done.1.gb, bf16[256,128]{1,0:T(8,128)(2,1)S(1)} %get-tuple-element.17.c.codes, ...), custom_call_target="tpu_custom_call" | custom-call | flops 1610612736 | bytes 20971520 | tf_op jit(solution)/shard_map/pallas_call | solution.py:139
  149.2 0.0 reduce-scatter.5.cloned.1.call-update
  149.3 0.1 collective-permute-start.2
  149.3 1.0 collective-permute-start.3
  150.4 0.0 copy-start.8
  150.4 1.2 copy-done.8
  151.6 12.7 %shard_map.112 = f32[256,4096]{1,0:T(8,128)S(1)} custom-call(s32[4,16]{1,0:T(4,128)S(1)} %select_reduce_fusion.table, bf16[256,4096]{1,0:T(8,128)(2,1)S(1)} %copy-done.2, bf16[256,4096]{1,0:T(8,128)(2,1)S(1)} %copy-done.2, bf16[64,256,256]{2,1,0:T(8,128)(2,1)} %wb.3, bf16[64,256,256]{2,1,0:T(8,128)(2,1)} %wb.3, ...), custom_call_target="tpu_custom_call" | custom-call | flops 1073741824 | bytes 12582912 | tf_op jit(solution)/shard_map/pallas_call | solution.py:85
  164.3 72.3 %collective-permute-done.2 = bf16[256,4096]{1,0:T(8,128)(2,1)S(1)} collective-permute-done((bf16[256,4096]{1,0:T(8,128)(2,1)}, bf16[256,4096]{1,0:T(8,128)(2,1)S(1)}, u32[]{:S(2)}, u32[]{:S(2)}) %collective-permute-start.2) | collective-permute-done | bytes 2097184 | tf_op jit(solution)/shard_map/ppermute | solution.py:38
  236.6 1.6 collective-permute-done.3
  238.2 2.3 add_convert_fusion
  240.5 0.0 reduce-scatter.3.cloned.1.call-done
  240.5 6.5 %reduce-scatter.5.cloned.1.call-done = f32[1,16,3,64,256]{4,3,2,1,0:T(8,128)} async-done(((f32[4,16,3,64,256]{4,3,2,1,0:T(8,128)}), f32[1,16,3,64,256]{4,3,2,1,0:T(8,128)}) %reduce-scatter.5.cloned.1.call-update) | async-done | bytes 3145744 | tf_op jit(solution)/shard_map/reduce_scatter | solution.py:208
  247.0 0.0 copy-start.9
  247.0 1.9 copy-done.9
  248.9 0.0 copy-start.10
  248.9 1.6 copy-done.10
  250.5 5.2 %shard_map.115 = (f32[64,64,256]{2,1,0:T(8,128)}, f32[32,4096]{1,0:T(8,128)}, f32[32,4096]{1,0:T(8,128)}) custom-call(s32[4,16]{1,0:T(4,128)S(1)} %select_reduce_fusion.table, f32[16,2,64,256]{3,2,1,0:T(8,128)S(1)} %bitcast.7, f32[16,3,64,256]{3,2,1,0:T(8,128)S(1)} %bitcast.6), custom_call_target="tpu_custom_call" | custom-call | bytes 10485760 | tf_op jit(solution)/shard_map/pallas_call | solution.py:163
  (2 shorter events, 0.0 us)
Async XLA Ops:
  7.2 18.4 %copy-start = (bf16[128,4096]{1,0:T(8,128)(2,1)S(1)}, bf16[128,4096]{1,0:T(8,128)(2,1)}, u32[]{:S(2)}) copy-start(bf16[128,4096]{1,0:T(8,128)(2,1)} %param.13) | copy-start | bytes 3145732
  7.2 233.4 %reduce-scatter.3.cloned.1.call-start = ((), (), s32[]{:S(2)}) async-start(), calls=%async_computation.2 | async-start | bytes 10485760 | tf_op jit(solution)/shard_map/reduce_scatter | solution.py:200
  7.2 1.7 copy-start.1
  8.9 1.6 copy-start.3
  16.4 3.4 %copy-start.6 = (f32[4,16,2,64,256]{4,3,2,1,0:T(8,128)}, f32[4,16,2,64,256]{4,3,2,1,0:T(8,128)S(1)}, u32[]{:S(2)}) copy-start(f32[4,16,2,64,256]{4,3,2,1,0:T(8,128)S(1)} %shard_map.113) | copy-start | bytes 25165828
  19.8 5.8 %copy-start.2 = (bf16[256,4096]{1,0:T(8,128)(2,1)S(1)}, bf16[256,4096]{1,0:T(8,128)(2,1)}, u32[]{:S(2)}) copy-start(bf16[256,4096]{1,0:T(8,128)(2,1)} %x.7) | copy-start | bytes 6291460
  19.8 227.2 %reduce-scatter.5.cloned.1.call-start = ((), (), s32[]{:S(2)}) async-start(), calls=%async_computation.3 | async-start | bytes 15728640 | tf_op jit(solution)/shard_map/reduce_scatter | solution.py:208
  19.9 6.4 %copy-start.4 = (bf16[256,4096]{1,0:T(8,128)(2,1)S(1)}, bf16[256,4096]{1,0:T(8,128)(2,1)}, u32[]{:S(2)}) copy-start(bf16[256,4096]{1,0:T(8,128)(2,1)} %g.3) | copy-start | bytes 6291460
  19.9 6.4 %copy-start.7 = (bf16[128,4096]{1,0:T(8,128)(2,1)S(1)}, bf16[128,4096]{1,0:T(8,128)(2,1)}, u32[]{:S(2)}) copy-start(bf16[128,4096]{1,0:T(8,128)(2,1)} %low.1) | copy-start | bytes 3145732
  19.9 113.5 %collective-permute-start.1 = (bf16[256,4096]{1,0:T(8,128)(2,1)}, bf16[256,4096]{1,0:T(8,128)(2,1)}, u32[]{:S(2)}, u32[]{:S(2)}) collective-permute-start(bf16[256,4096]{1,0:T(8,128)(2,1)} %g.3), channel_id=1, source_target_pairs={{0,8},{8,0},{4,12},{12,4},{1,9},{9,1},{5,13},{13,5},{2,10},{10,2},... | collective-permute-start | bytes 6291464 | tf_op jit(solution)/shard_map/ppermute | solution.py:38
  24.0 109.4 %collective-permute-start = (bf16[256,4096]{1,0:T(8,128)(2,1)}, bf16[256,4096]{1,0:T(8,128)(2,1)}, u32[]{:S(2)}, u32[]{:S(2)}) collective-permute-start(bf16[256,4096]{1,0:T(8,128)(2,1)} %g.3), channel_id=1, source_target_pairs={{0,4},{4,0},{8,12},{12,8},{1,5},{5,1},{9,13},{13,9},{2,6},{6,2},{1... | collective-permute-start | bytes 6291464 | tf_op jit(solution)/shard_map/ppermute | solution.py:38
  26.3 0.8 copy-start.13
  26.3 0.7 copy-start.14
  26.3 0.8 copy-start.15
  39.5 1.3 copy-start.11
  40.8 1.3 copy-start.12
  133.4 1.6 copy-start.5
  149.3 87.4 %collective-permute-start.2 = (bf16[256,4096]{1,0:T(8,128)(2,1)}, bf16[256,4096]{1,0:T(8,128)(2,1)S(1)}, u32[]{:S(2)}, u32[]{:S(2)}) collective-permute-start(bf16[256,4096]{1,0:T(8,128)(2,1)} %copy-done.12), channel_id=1, source_target_pairs={{0,4},{4,0},{8,12},{12,8},{1,5},{5,1},{9,13},{13,9},{2,6},{6,2},{1... | collective-permute-start | bytes 6291464 | tf_op jit(solution)/shard_map/ppermute | solution.py:38
  149.3 88.9 %collective-permute-start.3 = (bf16[256,4096]{1,0:T(8,128)(2,1)}, bf16[256,4096]{1,0:T(8,128)(2,1)S(1)}, u32[]{:S(2)}, u32[]{:S(2)}) collective-permute-start(bf16[256,4096]{1,0:T(8,128)(2,1)} %copy-done.11), channel_id=1, source_target_pairs={{0,8},{8,0},{4,12},{12,4},{1,9},{9,1},{5,13},{13,5},{2,10},{10,2},... | collective-permute-start | bytes 6291464 | tf_op jit(solution)/shard_map/ppermute | solution.py:38
  150.4 1.2 copy-start.8
  247.0 1.9 copy-start.9
  248.9 1.6 copy-start.10
Sparse Core Ops, SparseCore 0:
  19.9 74.4 reduce-scatter.2
  149.4 97.5 reduce-scatter.4

commit v2 on v1

--- a/solution.py
+++ b/solution.py
@@ -126,10 +126,10 @@
 def far_grad_kernel(n, x, g, ga, gb, codes, backs, o):
     part = BLOCK // n
     half = part // 2
-    o[:, 0, 0] = dot(ga[...], x[...], TN).reshape(n, part, BLOCK)
-    o[:, 0, 1] = dot(gb[...], x[...], TN).reshape(n, part, BLOCK)
-    o[:, 0, 2, :half] = dot(backs[...], x[...], TN).reshape(n, half, BLOCK)
-    o[:, 0, 2, half:] = dot(codes[...], g[...], TN).reshape(n, half, BLOCK)
+    o[:, 0, 0] = dot(ga[...], x[...], TN).astype(BF16).reshape(n, part, BLOCK)
+    o[:, 0, 1] = dot(gb[...], x[...], TN).astype(BF16).reshape(n, part, BLOCK)
+    o[:, 0, 2, :half] = dot(backs[...], x[...], TN).astype(BF16).reshape(n, half, BLOCK)
+    o[:, 0, 2, half:] = dot(codes[...], g[...], TN).astype(BF16).reshape(n, half, BLOCK)
 
 
 def far_grads(n, features, cotangent, from_a, from_b, codes, backs):
@@ -139,7 +139,7 @@
     return pl.pallas_call(
         functools.partial(far_grad_kernel, n),
         grid=(share,),
-        out_shape=jax.ShapeDtypeStruct((n, share, 3, BLOCK // n, BLOCK), F32),
+        out_shape=jax.ShapeDtypeStruct((n, share, 3, BLOCK // n, BLOCK), BF16),
         in_specs=[column(rows)] * 4 + [whole] * 2,
         out_specs=pl.BlockSpec((n, 1, 3, BLOCK // n, BLOCK), lambda j: (0, j, 0, 0, 0)),
         compiler_params=params(),
@@ -151,10 +151,10 @@
     half = grad_in.shape[0]
     for j in range(share):
         for s in range(4):
-            value = near[j, s] if s < 2 else far[j, s - 2]
+            value = near[j, s] if s < 2 else far[j, s - 2].astype(F32)
             blocks[:, pl.ds(table[s, j], 1), :] = value[:, None, :]
-        grad_in[:, j * BLOCK : (j + 1) * BLOCK] = far[j, 2, :half]
-        grad_out[:, j * BLOCK : (j + 1) * BLOCK] = far[j, 2, half:]
+        grad_in[:, j * BLOCK : (j + 1) * BLOCK] = far[j, 2, :half].astype(F32)
+        grad_out[:, j * BLOCK : (j + 1) * BLOCK] = far[j, 2, half:].astype(F32)
 
 
 def place(table, near, far):
@@ -191,6 +191,7 @@
 
     from_a = swapped(cotangent, "wloop", top_bit - 2)
     from_b = swapped(cotangent, "wloop", top_bit - 1)
+    to_a, to_b = far_partials(table, features, block_weights)
     near = near_grads(items, features, cotangent)
     partial_code = dot(features, lowrank_in, NT)
     partial_back = dot(cotangent, lowrank_out, NT)
@@ -198,13 +199,13 @@
     codes = codes.astype(BF16)
     backs = backs.astype(BF16)
     near_share = lax.psum_scatter(near, "items", scatter_dimension=0, tiled=True)[0]
-    to_a, to_b = far_partials(table, features, block_weights)
     to_a, to_b, from_a, from_b, codes, backs = lax.optimization_barrier(
         (to_a, to_b, from_a, from_b, codes, backs)
     )
     got_a = swapped(to_a, "wloop", top_bit - 2)
     got_b = swapped(to_b, "wloop", top_bit - 1)
     far = far_grads(items, features, cotangent, from_a, from_b, codes, backs)
+    far, near_share = lax.optimization_barrier((far, near_share))
     far_share = lax.psum_scatter(far, "items", scatter_dimension=0, tiled=True)[0]
     total = near_total(table, features, block_weights, codes, lowrank_out)
     block_grads, grad_in, grad_out = place(table, near_share, far_share)

time: 264 us -> 254 us (0.962)
  waiting for transfers between devices: 80.4 us -> 74.3 us
    reduce_scatter x1, waiting for transfers between devices: 6.46 us -> 0.01 us  [body(): lax.psum_scatter(far, 'items', scatter_dimension=0, tiled=True)[0]]
  transfers between devices with their start and end apart: 6 -> 6, of which waited for: 3 -> 2; matrix products, arithmetic and copies ran while one was open for 2% -> 2% of each run, Pallas kernels for 15% -> 15%
where the time goes in v2:
time: 254 us; the launch traced here: 253 us
  blocking collectives  91.3 us (36%)
  waiting for transfers between devices  74.3 us (29%)
  Pallas kernels  48.6 us (19%)
  between operations  14.3 us (6%)
  local copies, waits for them, and re-layouts  13.4 us (5%)
  starting transfers between devices  6.84 us (3%)
  other arithmetic  2.57 us (1%)
    psum x1, blocking collectives, body(): codes, backs = lax.psum((partial_code, partial_back), 'wloop')  91.3 us
    ppermute x4, waiting for transfers between devices, swapped(): return lax.ppermute(block, axis, route)  74.2 us
    unnamed x32, local copies, waits for them, and re-layouts  13.4 us
    pallas_call x1, Pallas kernels, far_grads(): pl.pallas_call(functools.partial(far_grad_kernel, n), grid=(share,), out_...  13 us
    pallas_call x1, Pallas kernels, near_total(): pl.pallas_call(near_kernel, out_shape=jax.ShapeDtypeStruct((rows, width),...  12.4 us
    pallas_call x1, Pallas kernels, far_partials(): pl.pallas_call(far_kernel, out_shape=[jax.ShapeDtypeStruct((rows, width),...  12.1 us
    ppermute x4, starting transfers between devices, swapped(): return lax.ppermute(block, axis, route)  6.76 us
    pallas_call x1, Pallas kernels, near_grads(): pl.pallas_call(functools.partial(near_grad_kernel, n), grid=(share,), out...  5.91 us
  transfers between devices with their start and end apart: 6, of which 2 were waited for; matrix products, arithmetic and copies ran while one was open for 2% of the time, Pallas kernels for 15%

profile of v2, /device:TPU:0, one launch (start us, length us, event | category | flops | bytes accessed | tf_op | source)
XLA Modules:
  0.0 252.7 jit_solution(17966658653257429085)
XLA Ops:
  7.2 0.0 copy-start
  7.2 0.0 reduce-scatter.3.cloned.1.call-start
  7.2 0.0 copy-start.1
  7.2 1.7 copy-done.1
  8.9 0.0 copy-start.3
  8.9 1.6 copy-done.3
  10.5 5.9 %shard_map.114 = f32[4,16,2,64,256]{4,3,2,1,0:T(8,128)S(1)} custom-call(bf16[256,4096]{1,0:T(8,128)(2,1)S(1)} %copy-done.1, bf16[256,4096]{1,0:T(8,128)(2,1)S(1)} %copy-done.3, bf16[256,4096]{1,0:T(8,128)(2,1)S(1)} %copy-done.3), custom_call_target="tpu_custom_call" | custom-call | flops 1073741824 | bytes 14680064 | tf_op jit(solution)/shard_map/pallas_call | solution.py:115
  16.4 0.0 copy-start.6
  16.4 3.2 %copy-done.6 = f32[4,16,2,64,256]{4,3,2,1,0:T(8,128)} copy-done((f32[4,16,2,64,256]{4,3,2,1,0:T(8,128)}, f32[4,16,2,64,256]{4,3,2,1,0:T(8,128)S(1)}, u32[]{:S(2)}) %copy-start.6) | copy-done | bytes 8388632
  19.6 0.0 copy-start.2
  19.6 0.0 reduce-scatter.3.cloned.1.call-update
  19.7 0.0 reduce-scatter.5.cloned.1.call-start
  19.7 0.0 copy-start.4
  19.7 0.0 copy-start.7
  19.7 4.1 %collective-permute-start.1 = (bf16[256,4096]{1,0:T(8,128)(2,1)}, bf16[256,4096]{1,0:T(8,128)(2,1)}, u32[]{:S(2)}, u32[]{:S(2)}) collective-permute-start(bf16[256,4096]{1,0:T(8,128)(2,1)} %h.1), channel_id=1, source_target_pairs={{0,8},{8,0},{4,12},{12,4},{1,9},{9,1},{5,13},{13,5},{2,10},{10,2},... | collective-permute-start | bytes 6291464 | tf_op jit(solution)/shard_map/ppermute | solution.py:38
  23.9 1.6 collective-permute-start
  25.4 0.0 copy-done
  25.4 0.0 copy-done.2
  25.4 0.7 fusion.1
  26.1 0.0 copy-done.4
  26.1 0.0 copy-done.7
  26.2 0.0 copy-start.13
  26.2 0.0 copy-start.14
  26.2 0.0 copy-start.15
  26.2 0.7 fusion.2
  26.9 0.0 copy-done.13
  26.9 0.0 copy-done.14
  26.9 0.0 copy-done.15
  27.0 0.1 broadcast_compare_fusion
  27.0 0.2 select_reduce_fusion.table
  27.2 12.1 %shard_map.111 = (bf16[256,4096]{1,0:T(8,128)(2,1)S(1)}, bf16[256,4096]{1,0:T(8,128)(2,1)S(1)}) custom-call(s32[4,16]{1,0:T(4,128)S(1)} %select_reduce_fusion.table, bf16[256,4096]{1,0:T(8,128)(2,1)S(1)} %copy-done.2, bf16[64,256,256]{2,1,0:T(8,128)(2,1)} %wb.3, bf16[64,256,256]{2,1,0:T(8,128)(2,1)} %wb.3), custom_call_target="tpu_custom_call" | custom-call | flops 1073741824 | bytes 10485760 | tf_op jit(solution)/shard_map/pallas_call | solution.py:65
  39.3 0.0 copy-start.11
  39.3 1.3 copy-done.11
  40.6 0.0 copy-start.12
  40.6 1.3 copy-done.12
  41.9 91.3 %all-reduce.2 = (bf16[256,128]{1,0:T(8,128)(2,1)S(1)}, bf16[256,128]{1,0:T(8,128)(2,1)S(1)}) all-reduce(f32[256,128]{1,0:T(8,128)S(1)} %fusion.1, f32[256,128]{1,0:T(8,128)S(1)} %fusion.2), channel_id=1, replica_groups=mesh['groups'=2,'wloop'=4,'items'=4] {'wloop'}, use_global_device_ids=true, to_apply=%region_1.2 | all-reduce | flops 65536 | bytes 393216 | tf_op jit(solution)/shard_map/psum | solution.py:198
  133.3 0.0 collective-permute-done.1.gb
  133.3 0.0 collective-permute-done.ga
  133.3 0.0 copy-start.5
  133.3 1.6 copy-done.5
  134.9 13.0 %shard_map.113 = bf16[4,16,3,64,256]{4,3,2,1,0:T(8,128)(2,1)} custom-call(bf16[256,4096]{1,0:T(8,128)(2,1)S(1)} %copy-done.2, bf16[256,4096]{1,0:T(8,128)(2,1)S(1)} %copy-done.5, bf16[256,4096]{1,0:T(8,128)(2,1)} %collective-permute-done.ga, bf16[256,4096]{1,0:T(8,128)(2,1)} %collective-permute-done.1.gb, bf16[256,128]{1,0:T(8,128)(2,1)S(1)} %get-tuple-element.19.c.codes, ...), custom_call_target="tpu_custom_call" | custom-call | flops 1610612736 | bytes 20971520 | tf_op jit(solution)/shard_map/pallas_call | solution.py:139
  147.9 0.0 reduce-scatter.3.cloned.1.call-done
  147.9 0.0 reduce-scatter.5.cloned.1.call-update
  147.9 0.1 collective-permute-start.2
  148.0 1.0 collective-permute-start.3
  149.0 0.0 copy-start.8
  149.0 1.2 copy-done.8
  150.2 12.4 %shard_map.112 = f32[256,4096]{1,0:T(8,128)S(1)} custom-call(s32[4,16]{1,0:T(4,128)S(1)} %select_reduce_fusion.table, bf16[256,4096]{1,0:T(8,128)(2,1)S(1)} %copy-done.2, bf16[256,4096]{1,0:T(8,128)(2,1)S(1)} %copy-done.2, bf16[64,256,256]{2,1,0:T(8,128)(2,1)} %wb.3, bf16[64,256,256]{2,1,0:T(8,128)(2,1)} %wb.3, ...), custom_call_target="tpu_custom_call" | custom-call | flops 1073741824 | bytes 12582912 | tf_op jit(solution)/shard_map/pallas_call | solution.py:85
  162.7 0.0 copy-start.9
  162.7 72.6 %collective-permute-done.2 = bf16[256,4096]{1,0:T(8,128)(2,1)S(1)} collective-permute-done((bf16[256,4096]{1,0:T(8,128)(2,1)}, bf16[256,4096]{1,0:T(8,128)(2,1)S(1)}, u32[]{:S(2)}, u32[]{:S(2)}) %collective-permute-start.2) | collective-permute-done | bytes 2097184 | tf_op jit(solution)/shard_map/ppermute | solution.py:38
  235.3 1.6 collective-permute-done.3
  236.9 2.3 add_convert_fusion
  239.2 0.0 reduce-scatter.5.cloned.1.call-done
  239.2 0.0 copy-done.9
  239.2 0.0 copy-start.10
  239.2 1.4 copy-done.10
  240.6 5.2 %shard_map.115 = (f32[64,64,256]{2,1,0:T(8,128)}, f32[32,4096]{1,0:T(8,128)}, f32[32,4096]{1,0:T(8,128)}) custom-call(s32[4,16]{1,0:T(4,128)S(1)} %select_reduce_fusion.table, f32[16,2,64,256]{3,2,1,0:T(8,128)S(1)} %bitcast.6, bf16[16,3,64,256]{3,2,1,0:T(8,128)(2,1)S(1)} %bitcast.7), custom_call_target="tpu_custom_call" | custom-call | bytes 10485760 | tf_op jit(solution)/shard_map/pallas_call | solution.py:163
  (2 shorter events, 0.0 us)
Async XLA Ops:
  7.2 18.3 %copy-start = (bf16[128,4096]{1,0:T(8,128)(2,1)S(1)}, bf16[128,4096]{1,0:T(8,128)(2,1)}, u32[]{:S(2)}) copy-start(bf16[128,4096]{1,0:T(8,128)(2,1)} %param.13) | copy-start | bytes 3145732
  7.2 140.7 %reduce-scatter.3.cloned.1.call-start = ((), (), s32[]{:S(2)}) async-start(), calls=%async_computation.2 | async-start | bytes 10485760 | tf_op jit(solution)/shard_map/reduce_scatter | solution.py:201
  7.2 1.7 copy-start.1
  8.9 1.6 copy-start.3
  16.4 3.2 %copy-start.6 = (f32[4,16,2,64,256]{4,3,2,1,0:T(8,128)}, f32[4,16,2,64,256]{4,3,2,1,0:T(8,128)S(1)}, u32[]{:S(2)}) copy-start(f32[4,16,2,64,256]{4,3,2,1,0:T(8,128)S(1)} %shard_map.114) | copy-start | bytes 25165828
  19.6 5.8 %copy-start.2 = (bf16[256,4096]{1,0:T(8,128)(2,1)S(1)}, bf16[256,4096]{1,0:T(8,128)(2,1)}, u32[]{:S(2)}) copy-start(bf16[256,4096]{1,0:T(8,128)(2,1)} %x.7) | copy-start | bytes 6291460
  19.7 219.6 %reduce-scatter.5.cloned.1.call-start = ((), (), s32[]{:S(2)}) async-start(), calls=%async_computation.3 | async-start | bytes 7864320 | tf_op jit(solution)/shard_map/reduce_scatter | solution.py:209
  19.7 6.4 %copy-start.4 = (bf16[256,4096]{1,0:T(8,128)(2,1)S(1)}, bf16[256,4096]{1,0:T(8,128)(2,1)}, u32[]{:S(2)}) copy-start(bf16[256,4096]{1,0:T(8,128)(2,1)} %h.1) | copy-start | bytes 6291460
  19.7 6.4 %copy-start.7 = (bf16[128,4096]{1,0:T(8,128)(2,1)S(1)}, bf16[128,4096]{1,0:T(8,128)(2,1)}, u32[]{:S(2)}) copy-start(bf16[128,4096]{1,0:T(8,128)(2,1)} %low.1) | copy-start | bytes 3145732
  19.7 113.5 %collective-permute-start.1 = (bf16[256,4096]{1,0:T(8,128)(2,1)}, bf16[256,4096]{1,0:T(8,128)(2,1)}, u32[]{:S(2)}, u32[]{:S(2)}) collective-permute-start(bf16[256,4096]{1,0:T(8,128)(2,1)} %h.1), channel_id=1, source_target_pairs={{0,8},{8,0},{4,12},{12,4},{1,9},{9,1},{5,13},{13,5},{2,10},{10,2},... | collective-permute-start | bytes 6291464 | tf_op jit(solution)/shard_map/ppermute | solution.py:38
  23.9 109.4 %collective-permute-start = (bf16[256,4096]{1,0:T(8,128)(2,1)}, bf16[256,4096]{1,0:T(8,128)(2,1)}, u32[]{:S(2)}, u32[]{:S(2)}) collective-permute-start(bf16[256,4096]{1,0:T(8,128)(2,1)} %h.1), channel_id=1, source_target_pairs={{0,4},{4,0},{8,12},{12,8},{1,5},{5,1},{9,13},{13,9},{2,6},{6,2},{1... | collective-permute-start | bytes 6291464 | tf_op jit(solution)/shard_map/ppermute | solution.py:38
  26.2 0.8 copy-start.13
  26.2 0.7 copy-start.14
  26.2 0.8 copy-start.15
  39.3 1.3 copy-start.11
  40.6 1.3 copy-start.12
  133.3 1.6 copy-start.5
  147.9 87.4 %collective-permute-start.2 = (bf16[256,4096]{1,0:T(8,128)(2,1)}, bf16[256,4096]{1,0:T(8,128)(2,1)S(1)}, u32[]{:S(2)}, u32[]{:S(2)}) collective-permute-start(bf16[256,4096]{1,0:T(8,128)(2,1)} %copy-done.12), channel_id=1, source_target_pairs={{0,4},{4,0},{8,12},{12,8},{1,5},{5,1},{9,13},{13,9},{2,6},{6,2},{1... | collective-permute-start | bytes 6291464 | tf_op jit(solution)/shard_map/ppermute | solution.py:38
  148.0 88.9 %collective-permute-start.3 = (bf16[256,4096]{1,0:T(8,128)(2,1)}, bf16[256,4096]{1,0:T(8,128)(2,1)S(1)}, u32[]{:S(2)}, u32[]{:S(2)}) collective-permute-start(bf16[256,4096]{1,0:T(8,128)(2,1)} %copy-done.11), channel_id=1, source_target_pairs={{0,8},{8,0},{4,12},{12,4},{1,9},{9,1},{5,13},{13,5},{2,10},{10,2},... | collective-permute-start | bytes 6291464 | tf_op jit(solution)/shard_map/ppermute | solution.py:38
  149.0 1.2 copy-start.8
  162.7 76.6 %copy-start.9 = (f32[1,16,2,64,256]{4,3,2,1,0:T(8,128)S(1)}, f32[1,16,2,64,256]{4,3,2,1,0:T(8,128)}, u32[]{:S(2)}) copy-start(f32[1,16,2,64,256]{4,3,2,1,0:T(8,128)} %reduce-scatter.3.cloned.1.call-done) | copy-start | bytes 6291460
  239.2 1.4 copy-start.10
Sparse Core Ops, SparseCore 0:
  19.8 74.4 reduce-scatter.2
  148.0 56.8 reduce-scatter.4

commit v3 on v2

--- a/solution.py
+++ b/solution.py
@@ -103,24 +103,24 @@
     )(table, features, features, weights, weights, codes, lowrank_out)
 
 
-def near_grad_kernel(n, x, g, h, o):
+def near_grad_kernel(n, table, x, g, h, o):
     part = BLOCK // n
     o[:, 0, 0] = dot(g[...], x[...], TN).reshape(n, part, BLOCK)
     o[:, 0, 1] = dot(h[...], x[...], TN).reshape(n, part, BLOCK)
 
 
-def near_grads(n, features, cotangent):
+def near_grads(table, n, features, cotangent):
     rows, width = features.shape
     share = width // BLOCK
     return pl.pallas_call(
         functools.partial(near_grad_kernel, n),
         grid=(share,),
         out_shape=jax.ShapeDtypeStruct((n, share, 2, BLOCK // n, BLOCK), F32),
-        in_specs=[column(rows), column(rows), paired(rows)],
+        in_specs=[pl.BlockSpec(memory_space=pltpu.SMEM), column(rows), column(rows), paired(rows)],
         out_specs=pl.BlockSpec((n, 1, 2, BLOCK // n, BLOCK), lambda j: (0, j, 0, 0, 0)),
         compiler_params=params(),
         cost_estimate=cost(4 * rows * width * BLOCK, 6 * rows * width + 8 * width * BLOCK),
-    )(features, cotangent, cotangent)
+    )(table, features, cotangent, cotangent)
 
 
 def far_grad_kernel(n, x, g, ga, gb, codes, backs, o):
@@ -192,9 +192,10 @@
     from_a = swapped(cotangent, "wloop", top_bit - 2)
     from_b = swapped(cotangent, "wloop", top_bit - 1)
     to_a, to_b = far_partials(table, features, block_weights)
-    near = near_grads(items, features, cotangent)
     partial_code = dot(features, lowrank_in, NT)
     partial_back = dot(cotangent, lowrank_out, NT)
+    partial_code, partial_back, later = lax.optimization_barrier((partial_code, partial_back, table))
+    near = near_grads(later, items, features, cotangent)
     codes, backs = lax.psum((partial_code, partial_back), "wloop")
     codes = codes.astype(BF16)
     backs = backs.astype(BF16)

time: 254 us -> 257 us (1.012)
    unnamed x32 -> x22, local copies, waits for them, and re-layouts: 13.4 us -> 11 us
  transfers between devices with their start and end apart: 6 -> 6, of which waited for: 2 -> 2; matrix products, arithmetic and copies ran while one was open for 2% -> 1% of each run, Pallas kernels for 15% -> 15%
where the time goes in v3:
time: 257 us; the launch traced here: 256 us
  blocking collectives  93.1 us (36%)
  waiting for transfers between devices  74.3 us (29%)
  Pallas kernels  49.3 us (19%)
  between operations  14.2 us (6%)
  local copies, waits for them, and re-layouts  11 us (4%)
  starting transfers between devices  6.84 us (3%)
  other arithmetic  4.41 us (2%)
  matrix products  3.01 us (1%)
    psum x1, blocking collectives, body(): codes, backs = lax.psum((partial_code, partial_back), 'wloop')  93.1 us
    ppermute x4, waiting for transfers between devices, swapped(): return lax.ppermute(block, axis, route)  74.2 us
    pallas_call x1, Pallas kernels, far_grads(): pl.pallas_call(functools.partial(far_grad_kernel, n), grid=(share,), out_...  13 us
    pallas_call x1, Pallas kernels, near_total(): pl.pallas_call(near_kernel, out_shape=jax.ShapeDtypeStruct((rows, width),...  12.5 us
    pallas_call x1, Pallas kernels, far_partials(): pl.pallas_call(far_kernel, out_shape=[jax.ShapeDtypeStruct((rows, width),...  12.1 us
    unnamed x22, local copies, waits for them, and re-layouts  11 us
    ppermute x4, starting transfers between devices, swapped(): return lax.ppermute(block, axis, route)  6.76 us
    pallas_call x1, Pallas kernels, near_grads(): pl.pallas_call(functools.partial(near_grad_kernel, n), grid=(share,), out...  6.56 us
  transfers between devices with their start and end apart: 6, of which 2 were waited for; matrix products, arithmetic and copies ran while one was open for 1% of the time, Pallas kernels for 15%

profile of v3, /device:TPU:0, one launch (start us, length us, event | category | flops | bytes accessed | tf_op | source)
XLA Modules:
  0.0 256.1 jit_solution(1480130173358332482)
XLA Ops:
  7.2 0.0 copy-start
  7.2 0.0 reduce-scatter.3.cloned.1.call-start
  7.2 0.0 copy-start.3
  7.2 0.0 copy-start.5
  7.3 0.8 and_select_fusion
  8.1 1.1 broadcast_compare_fusion
  9.2 0.2 select_reduce_fusion.table
  9.3 0.0 copy-done
  9.4 2.3 fusion.1
  11.7 0.0 copy-done.3
  11.7 0.0 copy-done.5
  11.7 0.0 copy-start.1
  11.7 0.7 fusion.2
  12.4 0.9 copy-done.1
  13.3 6.6 %shard_map.114 = f32[4,16,2,64,256]{4,3,2,1,0:T(8,128)S(1)} custom-call(s32[4,16]{1,0:T(4,128)S(1)} %select_reduce_fusion.table, bf16[256,4096]{1,0:T(8,128)(2,1)S(1)} %copy-done.1, bf16[256,4096]{1,0:T(8,128)(2,1)S(1)} %copy-done.3, bf16[256,4096]{1,0:T(8,128)(2,1)S(1)} %copy-done.3), custom_call_target="tpu_custom_call" | custom-call | flops 1073741824 | bytes 14680064 | tf_op jit(solution)/shard_map/pallas_call | solution.py:115
  19.8 0.0 copy-start.2
  19.9 3.2 %copy-done.2 = f32[4,16,2,64,256]{4,3,2,1,0:T(8,128)} copy-done((f32[4,16,2,64,256]{4,3,2,1,0:T(8,128)}, f32[4,16,2,64,256]{4,3,2,1,0:T(8,128)S(1)}, u32[]{:S(2)}) %copy-start.2) | copy-done | bytes 8388632
  23.1 0.0 reduce-scatter.3.cloned.1.call-update
  23.1 0.0 reduce-scatter.5.cloned.1.call-start
  23.1 4.1 %collective-permute-start.1 = (bf16[256,4096]{1,0:T(8,128)(2,1)}, bf16[256,4096]{1,0:T(8,128)(2,1)}, u32[]{:S(2)}, u32[]{:S(2)}) collective-permute-start(bf16[256,4096]{1,0:T(8,128)(2,1)} %h.1), channel_id=1, source_target_pairs={{0,8},{8,0},{4,12},{12,4},{1,9},{9,1},{5,13},{13,5},{2,10},{10,2},... | collective-permute-start | bytes 6291464 | tf_op jit(solution)/shard_map/ppermute | solution.py:38
  27.3 1.6 collective-permute-start
  28.8 12.1 %shard_map.111 = (bf16[256,4096]{1,0:T(8,128)(2,1)S(1)}, bf16[256,4096]{1,0:T(8,128)(2,1)S(1)}) custom-call(s32[4,16]{1,0:T(4,128)S(1)} %select_reduce_fusion.table, bf16[256,4096]{1,0:T(8,128)(2,1)S(1)} %copy-done.1, bf16[64,256,256]{2,1,0:T(8,128)(2,1)} %wb.3, bf16[64,256,256]{2,1,0:T(8,128)(2,1)} %wb.3), custom_call_target="tpu_custom_call" | custom-call | flops 1073741824 | bytes 10485760 | tf_op jit(solution)/shard_map/pallas_call | solution.py:65
  41.0 0.0 copy-start.9
  41.0 1.3 copy-done.9
  42.3 0.0 copy-start.10
  42.3 1.3 copy-done.10
  43.6 93.1 %all-reduce.2 = (bf16[256,128]{1,0:T(8,128)(2,1)S(1)}, bf16[256,128]{1,0:T(8,128)(2,1)S(1)}) all-reduce(f32[256,128]{1,0:T(8,128)S(1)} %fusion.1, f32[256,128]{1,0:T(8,128)S(1)} %fusion.2), channel_id=1, replica_groups=mesh['groups'=2,'wloop'=4,'items'=4] {'wloop'}, use_global_device_ids=true, to_apply=%region_1.2 | all-reduce | flops 65536 | bytes 393216 | tf_op jit(solution)/shard_map/psum | solution.py:199
  136.7 0.0 collective-permute-done.1.gb
  136.7 0.0 collective-permute-done.ga
  136.7 0.0 copy-start.4
  136.7 1.6 copy-done.4
  138.3 13.0 %shard_map.113 = bf16[4,16,3,64,256]{4,3,2,1,0:T(8,128)(2,1)} custom-call(bf16[256,4096]{1,0:T(8,128)(2,1)S(1)} %copy-done.1, bf16[256,4096]{1,0:T(8,128)(2,1)S(1)} %copy-done.4, bf16[256,4096]{1,0:T(8,128)(2,1)} %collective-permute-done.ga, bf16[256,4096]{1,0:T(8,128)(2,1)} %collective-permute-done.1.gb, bf16[256,128]{1,0:T(8,128)(2,1)S(1)} %get-tuple-element.24.c.codes, ...), custom_call_target="tpu_custom_call" | custom-call | flops 1610612736 | bytes 20971520 | tf_op jit(solution)/shard_map/pallas_call | solution.py:139
  151.3 0.0 reduce-scatter.3.cloned.1.call-done
  151.3 0.0 reduce-scatter.5.cloned.1.call-update
  151.3 0.1 collective-permute-start.2
  151.4 1.0 collective-permute-start.3
  152.4 0.0 copy-start.6
  152.4 1.2 copy-done.6
  153.7 12.5 %shard_map.112 = f32[256,4096]{1,0:T(8,128)S(1)} custom-call(s32[4,16]{1,0:T(4,128)S(1)} %select_reduce_fusion.table, bf16[256,4096]{1,0:T(8,128)(2,1)S(1)} %copy-done.1, bf16[256,4096]{1,0:T(8,128)(2,1)S(1)} %copy-done.1, bf16[64,256,256]{2,1,0:T(8,128)(2,1)} %wb.3, bf16[64,256,256]{2,1,0:T(8,128)(2,1)} %wb.3, ...), custom_call_target="tpu_custom_call" | custom-call | flops 1073741824 | bytes 12582912 | tf_op jit(solution)/shard_map/pallas_call | solution.py:85
  166.1 0.0 copy-start.7
  166.1 72.6 %collective-permute-done.2 = bf16[256,4096]{1,0:T(8,128)(2,1)S(1)} collective-permute-done((bf16[256,4096]{1,0:T(8,128)(2,1)}, bf16[256,4096]{1,0:T(8,128)(2,1)S(1)}, u32[]{:S(2)}, u32[]{:S(2)}) %collective-permute-start.2) | collective-permute-done | bytes 2097184 | tf_op jit(solution)/shard_map/ppermute | solution.py:38
  238.8 1.6 collective-permute-done.3
  240.3 2.3 add_convert_fusion
  242.7 0.0 reduce-scatter.5.cloned.1.call-done
  242.7 0.0 copy-done.7
  242.7 0.0 copy-start.8
  242.7 1.4 copy-done.8
  244.1 5.2 %shard_map.115 = (f32[64,64,256]{2,1,0:T(8,128)}, f32[32,4096]{1,0:T(8,128)}, f32[32,4096]{1,0:T(8,128)}) custom-call(s32[4,16]{1,0:T(4,128)S(1)} %select_reduce_fusion.table, f32[16,2,64,256]{3,2,1,0:T(8,128)S(1)} %bitcast.6, bf16[16,3,64,256]{3,2,1,0:T(8,128)(2,1)S(1)} %bitcast.7), custom_call_target="tpu_custom_call" | custom-call | bytes 10485760 | tf_op jit(solution)/shard_map/pallas_call | solution.py:163
  (1 shorter events, 0.0 us)
Async XLA Ops:
  7.2 2.2 copy-start
  7.2 144.1 %reduce-scatter.3.cloned.1.call-start = ((), (), s32[]{:S(2)}) async-start(), calls=%async_computation.2 | async-start | bytes 10485760 | tf_op jit(solution)/shard_map/reduce_scatter | solution.py:202
  7.2 4.4 %copy-start.3 = (bf16[256,4096]{1,0:T(8,128)(2,1)S(1)}, bf16[256,4096]{1,0:T(8,128)(2,1)}, u32[]{:S(2)}) copy-start(bf16[256,4096]{1,0:T(8,128)(2,1)} %h.1) | copy-start | bytes 6291460
  7.2 4.4 %copy-start.5 = (bf16[128,4096]{1,0:T(8,128)(2,1)S(1)}, bf16[128,4096]{1,0:T(8,128)(2,1)}, u32[]{:S(2)}) copy-start(bf16[128,4096]{1,0:T(8,128)(2,1)} %low.1) | copy-start | bytes 3145732
  11.7 1.6 copy-start.1
  19.8 3.2 %copy-start.2 = (f32[4,16,2,64,256]{4,3,2,1,0:T(8,128)}, f32[4,16,2,64,256]{4,3,2,1,0:T(8,128)S(1)}, u32[]{:S(2)}) copy-start(f32[4,16,2,64,256]{4,3,2,1,0:T(8,128)S(1)} %shard_map.114) | copy-start | bytes 25165828
  23.1 219.6 %reduce-scatter.5.cloned.1.call-start = ((), (), s32[]{:S(2)}) async-start(), calls=%async_computation.3 | async-start | bytes 7864320 | tf_op jit(solution)/shard_map/reduce_scatter | solution.py:210
  23.1 113.6 %collective-permute-start.1 = (bf16[256,4096]{1,0:T(8,128)(2,1)}, bf16[256,4096]{1,0:T(8,128)(2,1)}, u32[]{:S(2)}, u32[]{:S(2)}) collective-permute-start(bf16[256,4096]{1,0:T(8,128)(2,1)} %h.1), channel_id=1, source_target_pairs={{0,8},{8,0},{4,12},{12,4},{1,9},{9,1},{5,13},{13,5},{2,10},{10,2},... | collective-permute-start | bytes 6291464 | tf_op jit(solution)/shard_map/ppermute | solution.py:38
  27.3 109.5 %collective-permute-start = (bf16[256,4096]{1,0:T(8,128)(2,1)}, bf16[256,4096]{1,0:T(8,128)(2,1)}, u32[]{:S(2)}, u32[]{:S(2)}) collective-permute-start(bf16[256,4096]{1,0:T(8,128)(2,1)} %h.1), channel_id=1, source_target_pairs={{0,4},{4,0},{8,12},{12,8},{1,5},{5,1},{9,13},{13,9},{2,6},{6,2},{1... | collective-permute-start | bytes 6291464 | tf_op jit(solution)/shard_map/ppermute | solution.py:38
  41.0 1.3 copy-start.9
  42.3 1.3 copy-start.10
  136.7 1.6 copy-start.4
  151.3 87.4 %collective-permute-start.2 = (bf16[256,4096]{1,0:T(8,128)(2,1)}, bf16[256,4096]{1,0:T(8,128)(2,1)S(1)}, u32[]{:S(2)}, u32[]{:S(2)}) collective-permute-start(bf16[256,4096]{1,0:T(8,128)(2,1)} %copy-done.10), channel_id=1, source_target_pairs={{0,4},{4,0},{8,12},{12,8},{1,5},{5,1},{9,13},{13,9},{2,6},{6,2},{1... | collective-permute-start | bytes 6291464 | tf_op jit(solution)/shard_map/ppermute | solution.py:38
  151.4 88.9 %collective-permute-start.3 = (bf16[256,4096]{1,0:T(8,128)(2,1)}, bf16[256,4096]{1,0:T(8,128)(2,1)S(1)}, u32[]{:S(2)}, u32[]{:S(2)}) collective-permute-start(bf16[256,4096]{1,0:T(8,128)(2,1)} %copy-done.9), channel_id=1, source_target_pairs={{0,8},{8,0},{4,12},{12,4},{1,9},{9,1},{5,13},{13,5},{2,10},{10,2},... | collective-permute-start | bytes 6291464 | tf_op jit(solution)/shard_map/ppermute | solution.py:38
  152.4 1.2 copy-start.6
  166.1 76.6 %copy-start.7 = (f32[1,16,2,64,256]{4,3,2,1,0:T(8,128)S(1)}, f32[1,16,2,64,256]{4,3,2,1,0:T(8,128)}, u32[]{:S(2)}) copy-start(f32[1,16,2,64,256]{4,3,2,1,0:T(8,128)} %reduce-scatter.3.cloned.1.call-done) | copy-start | bytes 6291460
  242.7 1.4 copy-start.8
Sparse Core Ops, SparseCore 0:
  23.2 74.4 reduce-scatter.2
  151.5 56.8 reduce-scatter.4
